TPU v7x, 512 devices: a whole 4x4x16 slice. The times are simulated.
512 devices in a mesh: freq: 8 (over y, core), pair: 64 (over x, z).
Axes of the slice: x: 4, y: 4, z: 16, core: 2. Of those that a mesh axis runs over, the one named last changes fastest.
Arguments:
- spectra: bfloat16 [2, 24, 512, 16384], P(None, 'freq', None, 'pair'), may hold values from -6 to 6
- pair_blocks: int32 [1024, 2], P('pair'), may hold values from 0 to 127, as said below
- pair_valid: int32 [1024], P('pair'), may hold values from 0 to 1, as said below
Outputs:
- stack: float32 [512, 16384], P('freq', 'pair')
Inputs may be any that keep to these rules, and one draw needn't show every extreme that they name: `pair_blocks`: row r belongs to owner r // 16; its first block lies in [owner * 2, (owner + 1) * 2); its second block is at or after the first and at most 6 blocks after it, and this largest distance occurs in every draw. `pair_valid`: within each owner's 16 rows the ones come first; every owner has at least one, and some owner has all 16.
All inputs are finite; a program needn't handle non-finite values.
Results may differ from a plain program's by a relative error of at most 0.00082.
Values may be sent and summed in bfloat16 or wider, within the bound.
A program may use at most 64 MiB of HBM per device.

v0:
```python
import jax
import jax.numpy as jnp
from jax import lax
from jax.sharding import PartitionSpec as P

SB = 128
HALF = 64
DEPTH = 3


EPS = 1e-06


def shifted(value, axis, by):
    devices = lax.axis_size(axis)
    pairs = [(i, i + by) for i in range(devices) if 0 <= i + by < devices]
    return lax.ppermute(value, axis, pairs)


def whiten(spectra):
    spectra_f32 = spectra.astype(jnp.float32)
    magnitude = jnp.sqrt(spectra_f32[0] * spectra_f32[0] + spectra_f32[1] * spectra_f32[1])
    freq_bins = jnp.arange(spectra_f32.shape[2])
    window = (jnp.abs(freq_bins[:, None] - freq_bins[None, :]) <= HALF).astype(jnp.float32)
    counted = jnp.sum(window, axis=1)
    smooth = (
        jnp.einsum("fg,wgs->wfs", window, magnitude, precision=lax.Precision.HIGHEST)
        / counted[None, :, None]
    )
    return (spectra_f32 / (smooth + EPS)[None]).astype(jnp.bfloat16)


def coherence_sums(left_block, right_block, scale):
    win_count = left_block.shape[1]
    freq_count = left_block.shape[2]
    block_size = left_block.shape[3]
    piece_bins = min(freq_count, 16)
    stacked_left = left_block.reshape(2 * win_count, freq_count, block_size)
    stacked_right = jnp.stack(
        [
            right_block.reshape(2 * win_count, freq_count, block_size),
            jnp.concatenate([-right_block[1], right_block[0]], axis=0),
        ]
    )

    def one_piece(start):
        left_piece = lax.dynamic_slice_in_dim(stacked_left, start, piece_bins, 1)
        right_piece = lax.dynamic_slice_in_dim(stacked_right, start, piece_bins, 2)
        product = jnp.einsum(
            "kfi,pkfj->pfij", left_piece, right_piece, preferred_element_type=jnp.float32
        )
        modulus = jnp.sqrt(product[0] * product[0] + product[1] * product[1]) * scale
        return (jnp.sum(modulus, axis=2), jnp.sum(modulus, axis=1))

    row_sums, col_sums = lax.map(one_piece, jnp.arange(freq_count // piece_bins) * piece_bins)
    return (row_sums.reshape(freq_count, block_size), col_sums.reshape(freq_count, block_size))


def add_block(totals, index, values):
    current = lax.dynamic_index_in_dim(totals, index, 1, keepdims=False)
    return lax.dynamic_update_index_in_dim(totals, current + values, index, 1)


def body(spectra, pair_blocks, pair_valid):
    whitened = whiten(spectra)
    local_part = lax.all_to_all(whitened, "freq", split_axis=2, concat_axis=1, tiled=True)
    held_blocks = local_part.shape[3] // SB
    pieces = [local_part]
    for offset in range(1, DEPTH + 1):
        pieces.append(shifted(local_part, "pair", -offset))
    band_data = jnp.concatenate(pieces, axis=3)
    win_count = local_part.shape[1]
    freq_count = local_part.shape[2]
    band_blocks = band_data.shape[3] // SB
    blocks = band_data.reshape(2, win_count, freq_count, band_blocks, SB)
    first_held = lax.axis_index("pair") * held_blocks
    scale = 1.0 / (win_count * SB)

    def visit(slot_index, totals):
        left_index = pair_blocks[slot_index, 0] - first_held
        right_index = pair_blocks[slot_index, 1] - first_held
        weight = pair_valid[slot_index].astype(jnp.float32)
        left_block = lax.dynamic_index_in_dim(blocks, left_index, 3, keepdims=False)
        right_block = lax.dynamic_index_in_dim(blocks, right_index, 3, keepdims=False)
        row_sums, col_sums = coherence_sums(left_block, right_block, scale)
        totals = add_block(totals, left_index, weight * row_sums)
        return add_block(totals, right_index, weight * col_sums)

    start_totals = jnp.zeros((freq_count, band_blocks, SB), jnp.float32)
    totals = lax.fori_loop(0, pair_blocks.shape[0], visit, start_totals)
    owned = totals[:, :held_blocks]
    for offset in range(1, DEPTH + 1):
        later = totals[:, offset * held_blocks : (offset + 1) * held_blocks]
        owned = owned + shifted(later, "pair", offset)
    return owned.reshape(freq_count, held_blocks * SB)


def solution(mesh):
    in_specs = (P(None, "freq", None, "pair"), P("pair", None), P("pair"))
    out_specs = P("freq", "pair")
    return jax.shard_map(body, mesh=mesh, in_specs=in_specs, out_specs=out_specs, check_vma=False)
```

profile of v0, /device:TPU:7, one launch (start us, length us, event | category | flops | bytes accessed | tf_op | source)
XLA Modules:
  0.0 633.4 jit_solution(467175150222631373)
XLA Ops:
  10.0 25.7 %all_to_all.18 = bf16[2,3,512,256]{3,0,1,2:T(2,128)(2,1)S(1)} all-to-all(bf16[2,3,512,256]{3,0,1,2:T(2,128)(2,1)S(1)} %copy.46), channel_id=1, replica_groups=mesh['freq'=8,'pair'=64] {'freq'}, dimensions={2} | all-to-all | bytes 3145728 | tf_op jit(solution)/shard_map/all_to_all | solution.py:66
  36.1 11.4 %collective-permute-start = (bf16[2,24,64,256]{3,2,1,0:T(8,128)(2,1)S(1)}, bf16[2,24,64,256]{3,2,1,0:T(8,128)(2,1)}, u32[]{:S(2)}, u32[]{:S(2)}) collective-permute-start(bf16[2,24,64,256]{3,2,1,0:T(8,128)(2,1)S(1)} %bitcast.78), channel_id=1, source_target_pairs={{1,0},{2,1},{3,2},{4,3},{5,4},{6,5},{7,6},{8,7},{9,8},{10,9},{11,1... | collective-permute-start | bytes 4718600 | tf_op jit(solution)/shard_map/ppermute | solution.py:17
  50.6 4.9 collective-permute-start.2
  56.0 33.3 %collective-permute-done = bf16[2,24,64,256]{3,2,1,0:T(8,128)(2,1)} collective-permute-done((bf16[2,24,64,256]{3,2,1,0:T(8,128)(2,1)S(1)}, bf16[2,24,64,256]{3,2,1,0:T(8,128)(2,1)}, u32[]{:S(2)}, u32[]{:S(2)}) %collective-permute-start) | collective-permute-done | bytes 1572896 | tf_op jit(solution)/shard_map/ppermute | solution.py:17
  92.8 66.6 %collective-permute-done.1 = bf16[2,24,64,256]{3,2,1,0:T(8,128)(2,1)} collective-permute-done((bf16[2,24,64,256]{3,2,1,0:T(8,128)(2,1)S(1)}, bf16[2,24,64,256]{3,2,1,0:T(8,128)(2,1)}, u32[]{:S(2)}, u32[]{:S(2)}) %collective-permute-start.1) | collective-permute-done | bytes 1572896 | tf_op jit(solution)/shard_map/ppermute | solution.py:17
  162.9 85.7 %collective-permute-done.2 = bf16[2,24,64,256]{3,2,1,0:T(8,128)(2,1)} collective-permute-done((bf16[2,24,64,256]{3,2,1,0:T(8,128)(2,1)S(1)}, bf16[2,24,64,256]{3,2,1,0:T(8,128)(2,1)}, u32[]{:S(2)}, u32[]{:S(2)}) %collective-permute-start.2) | collective-permute-done | bytes 1572896 | tf_op jit(solution)/shard_map/ppermute | solution.py:17
  252.3 8.6 %pad_maximum_fusion.1 = bf16[2,24,64,8,128]{4,3,2,1,0:T(8,128)(2,1)S(1)} fusion(bf16[2,24,64,2,128]{4,3,2,1,0:T(2,128)(2,1)} %concatenate.22, bf16[2,24,64,2,128]{4,3,2,1,0:T(2,128)(2,1)} %concatenate.21, bf16[2,24,64,2,128]{4,3,2,1,0:T(2,128)(2,1)S(1)} %copy-done, bf16[2,24,64,2,128]{4,3,2,1,0:T(2,128)(2,1)S(1)} %concatenate.19), kind=kLoop, calls=%fused_computation.31 | loop fusion | flops 25165824 | bytes 12582912 | tf_op jit(solution)/shard_map/concatenate | solution.py:71
  265.3 352.6 %while.42 = (s32[]{:T(128)}, f32[64,8,128]{2,0,1:T(8,128)S(1)}, s32[16,2]{0,1:T(2,128)S(1)}, s32[]{:T(128)}, s32[16]{0:T(128)S(1)}, /*index=5*/bf16[2,24,64,8,12...) while((s32[]{:T(128)}, f32[64,8,128]{2,0,1:T(8,128)S(1)}, ...), condition=%wide.region_6.7_spmd, body=%wide.region_1.6_spmd.sunk | while | flops 53309456 | bytes 16957984 | solution.py:90
  270.8 15.2 %while.43 = (s32[]{:T(128)}, f32[4,16,128]{2,1,0:T(8,128)S(1)}, f32[4,16,128]{2,1,0:T(8,128)S(1)}, s32[4]{0:T(128)S(1)}, bf16[2,48,64,128]{3,2,1,0:T(8,128)(2,1)...) while((s32[]{:T(128)}, f32[4,16,128]{2,1,0:T(8,128)S(1)}, ...), condition=%wide.region_5.5_spmd, body=%wide.region_2.4_spmd.sunk | while | flops 51900420 | bytes 5619863 | solution.py:55
  292.8 15.2 %while.43 = (s32[]{:T(128)}, f32[4,16,128]{2,1,0:T(8,128)S(1)}, f32[4,16,128]{2,1,0:T(8,128)S(1)}, s32[4]{0:T(128)S(1)}, bf16[2,48,64,128]{3,2,1,0:T(8,128)(2,1)...) while((s32[]{:T(128)}, f32[4,16,128]{2,1,0:T(8,128)S(1)}, ...), condition=%wide.region_5.5_spmd, body=%wide.region_2.4_spmd.sunk | while | flops 51900420 | bytes 5619863 | solution.py:55
  314.9 15.2 %while.43 = (s32[]{:T(128)}, f32[4,16,128]{2,1,0:T(8,128)S(1)}, f32[4,16,128]{2,1,0:T(8,128)S(1)}, s32[4]{0:T(128)S(1)}, bf16[2,48,64,128]{3,2,1,0:T(8,128)(2,1)...) while((s32[]{:T(128)}, f32[4,16,128]{2,1,0:T(8,128)S(1)}, ...), condition=%wide.region_5.5_spmd, body=%wide.region_2.4_spmd.sunk | while | flops 51900420 | bytes 5619863 | solution.py:55
  336.9 15.2 %while.43 = (s32[]{:T(128)}, f32[4,16,128]{2,1,0:T(8,128)S(1)}, f32[4,16,128]{2,1,0:T(8,128)S(1)}, s32[4]{0:T(128)S(1)}, bf16[2,48,64,128]{3,2,1,0:T(8,128)(2,1)...) while((s32[]{:T(128)}, f32[4,16,128]{2,1,0:T(8,128)S(1)}, ...), condition=%wide.region_5.5_spmd, body=%wide.region_2.4_spmd.sunk | while | flops 51900420 | bytes 5619863 | solution.py:55
  358.9 15.2 %while.43 = (s32[]{:T(128)}, f32[4,16,128]{2,1,0:T(8,128)S(1)}, f32[4,16,128]{2,1,0:T(8,128)S(1)}, s32[4]{0:T(128)S(1)}, bf16[2,48,64,128]{3,2,1,0:T(8,128)(2,1)...) while((s32[]{:T(128)}, f32[4,16,128]{2,1,0:T(8,128)S(1)}, ...), condition=%wide.region_5.5_spmd, body=%wide.region_2.4_spmd.sunk | while | flops 51900420 | bytes 5619863 | solution.py:55
  381.0 15.2 %while.43 = (s32[]{:T(128)}, f32[4,16,128]{2,1,0:T(8,128)S(1)}, f32[4,16,128]{2,1,0:T(8,128)S(1)}, s32[4]{0:T(128)S(1)}, bf16[2,48,64,128]{3,2,1,0:T(8,128)(2,1)...) while((s32[]{:T(128)}, f32[4,16,128]{2,1,0:T(8,128)S(1)}, ...), condition=%wide.region_5.5_spmd, body=%wide.region_2.4_spmd.sunk | while | flops 51900420 | bytes 5619863 | solution.py:55
  403.0 15.2 %while.43 = (s32[]{:T(128)}, f32[4,16,128]{2,1,0:T(8,128)S(1)}, f32[4,16,128]{2,1,0:T(8,128)S(1)}, s32[4]{0:T(128)S(1)}, bf16[2,48,64,128]{3,2,1,0:T(8,128)(2,1)...) while((s32[]{:T(128)}, f32[4,16,128]{2,1,0:T(8,128)S(1)}, ...), condition=%wide.region_5.5_spmd, body=%wide.region_2.4_spmd.sunk | while | flops 51900420 | bytes 5619863 | solution.py:55
  425.0 15.2 %while.43 = (s32[]{:T(128)}, f32[4,16,128]{2,1,0:T(8,128)S(1)}, f32[4,16,128]{2,1,0:T(8,128)S(1)}, s32[4]{0:T(128)S(1)}, bf16[2,48,64,128]{3,2,1,0:T(8,128)(2,1)...) while((s32[]{:T(128)}, f32[4,16,128]{2,1,0:T(8,128)S(1)}, ...), condition=%wide.region_5.5_spmd, body=%wide.region_2.4_spmd.sunk | while | flops 51900420 | bytes 5619863 | solution.py:55
  447.1 15.2 %while.43 = (s32[]{:T(128)}, f32[4,16,128]{2,1,0:T(8,128)S(1)}, f32[4,16,128]{2,1,0:T(8,128)S(1)}, s32[4]{0:T(128)S(1)}, bf16[2,48,64,128]{3,2,1,0:T(8,128)(2,1)...) while((s32[]{:T(128)}, f32[4,16,128]{2,1,0:T(8,128)S(1)}, ...), condition=%wide.region_5.5_spmd, body=%wide.region_2.4_spmd.sunk | while | flops 51900420 | bytes 5619863 | solution.py:55
  469.1 15.2 %while.43 = (s32[]{:T(128)}, f32[4,16,128]{2,1,0:T(8,128)S(1)}, f32[4,16,128]{2,1,0:T(8,128)S(1)}, s32[4]{0:T(128)S(1)}, bf16[2,48,64,128]{3,2,1,0:T(8,128)(2,1)...) while((s32[]{:T(128)}, f32[4,16,128]{2,1,0:T(8,128)S(1)}, ...), condition=%wide.region_5.5_spmd, body=%wide.region_2.4_spmd.sunk | while | flops 51900420 | bytes 5619863 | solution.py:55
  491.2 15.2 %while.43 = (s32[]{:T(128)}, f32[4,16,128]{2,1,0:T(8,128)S(1)}, f32[4,16,128]{2,1,0:T(8,128)S(1)}, s32[4]{0:T(128)S(1)}, bf16[2,48,64,128]{3,2,1,0:T(8,128)(2,1)...) while((s32[]{:T(128)}, f32[4,16,128]{2,1,0:T(8,128)S(1)}, ...), condition=%wide.region_5.5_spmd, body=%wide.region_2.4_spmd.sunk | while | flops 51900420 | bytes 5619863 | solution.py:55
  513.2 15.2 %while.43 = (s32[]{:T(128)}, f32[4,16,128]{2,1,0:T(8,128)S(1)}, f32[4,16,128]{2,1,0:T(8,128)S(1)}, s32[4]{0:T(128)S(1)}, bf16[2,48,64,128]{3,2,1,0:T(8,128)(2,1)...) while((s32[]{:T(128)}, f32[4,16,128]{2,1,0:T(8,128)S(1)}, ...), condition=%wide.region_5.5_spmd, body=%wide.region_2.4_spmd.sunk | while | flops 51900420 | bytes 5619863 | solution.py:55
  535.2 15.2 %while.43 = (s32[]{:T(128)}, f32[4,16,128]{2,1,0:T(8,128)S(1)}, f32[4,16,128]{2,1,0:T(8,128)S(1)}, s32[4]{0:T(128)S(1)}, bf16[2,48,64,128]{3,2,1,0:T(8,128)(2,1)...) while((s32[]{:T(128)}, f32[4,16,128]{2,1,0:T(8,128)S(1)}, ...), condition=%wide.region_5.5_spmd, body=%wide.region_2.4_spmd.sunk | while | flops 51900420 | bytes 5619863 | solution.py:55
  557.3 15.2 %while.43 = (s32[]{:T(128)}, f32[4,16,128]{2,1,0:T(8,128)S(1)}, f32[4,16,128]{2,1,0:T(8,128)S(1)}, s32[4]{0:T(128)S(1)}, bf16[2,48,64,128]{3,2,1,0:T(8,128)(2,1)...) while((s32[]{:T(128)}, f32[4,16,128]{2,1,0:T(8,128)S(1)}, ...), condition=%wide.region_5.5_spmd, body=%wide.region_2.4_spmd.sunk | while | flops 51900420 | bytes 5619863 | solution.py:55
  579.3 15.2 %while.43 = (s32[]{:T(128)}, f32[4,16,128]{2,1,0:T(8,128)S(1)}, f32[4,16,128]{2,1,0:T(8,128)S(1)}, s32[4]{0:T(128)S(1)}, bf16[2,48,64,128]{3,2,1,0:T(8,128)(2,1)...) while((s32[]{:T(128)}, f32[4,16,128]{2,1,0:T(8,128)S(1)}, ...), condition=%wide.region_5.5_spmd, body=%wide.region_2.4_spmd.sunk | while | flops 51900420 | bytes 5619863 | solution.py:55
  601.4 15.2 %while.43 = (s32[]{:T(128)}, f32[4,16,128]{2,1,0:T(8,128)S(1)}, f32[4,16,128]{2,1,0:T(8,128)S(1)}, s32[4]{0:T(128)S(1)}, bf16[2,48,64,128]{3,2,1,0:T(8,128)(2,1)...) while((s32[]{:T(128)}, f32[4,16,128]{2,1,0:T(8,128)S(1)}, ...), condition=%wide.region_5.5_spmd, body=%wide.region_2.4_spmd.sunk | while | flops 51900420 | bytes 5619863 | solution.py:55
  (559 shorter events, 239.6 us)
Async XLA Ops:
  6.0 2.0 copy-start.1
  36.1 53.2 %collective-permute-start = (bf16[2,24,64,256]{3,2,1,0:T(8,128)(2,1)S(1)}, bf16[2,24,64,256]{3,2,1,0:T(8,128)(2,1)}, u32[]{:S(2)}, u32[]{:S(2)}) collective-permute-start(bf16[2,24,64,256]{3,2,1,0:T(8,128)(2,1)S(1)} %bitcast.78), channel_id=1, source_target_pairs={{1,0},{2,1},{3,2},{4,3},{5,4},{6,5},{7,6},{8,7},{9,8},{10,9},{11,1... | collective-permute-start | bytes 4718600 | tf_op jit(solution)/shard_map/ppermute | solution.py:17
  47.5 111.9 %collective-permute-start.1 = (bf16[2,24,64,256]{3,2,1,0:T(8,128)(2,1)S(1)}, bf16[2,24,64,256]{3,2,1,0:T(8,128)(2,1)}, u32[]{:S(2)}, u32[]{:S(2)}) collective-permute-start(bf16[2,24,64,256]{3,2,1,0:T(8,128)(2,1)S(1)} %bitcast.79), channel_id=1, source_target_pairs={{2,0},{3,1},{4,2},{5,3},{6,4},{7,5},{8,6},{9,7},{10,8},{11,9},{12,... | collective-permute-start | bytes 4718600 | tf_op jit(solution)/shard_map/ppermute | solution.py:17
  50.6 198.1 %collective-permute-start.2 = (bf16[2,24,64,256]{3,2,1,0:T(8,128)(2,1)S(1)}, bf16[2,24,64,256]{3,2,1,0:T(8,128)(2,1)}, u32[]{:S(2)}, u32[]{:S(2)}) collective-permute-start(bf16[2,24,64,256]{3,2,1,0:T(8,128)(2,1)S(1)} %bitcast.80), channel_id=1, source_target_pairs={{3,0},{4,1},{5,2},{6,3},{7,4},{8,5},{9,6},{10,7},{11,8},{12,9},{13... | collective-permute-start | bytes 4718600 | tf_op jit(solution)/shard_map/ppermute | solution.py:17
  248.7 3.6 copy-start
  260.9 4.4 copy-start.2
  260.9 4.4 copy-start.3
  617.9 8.6 %collective-permute-start.3 = (f32[64,2,128]{2,0,1:T(8,128)S(1)}, f32[64,2,128]{2,0,1:T(8,128)S(1)}, u32[]{:S(2)}, u32[]{:S(2)}) collective-permute-start(f32[64,2,128]{2,0,1:T(8,128)S(1)} %get-tuple-element.244), channel_id=1, source_target_pairs={{0,1},{1,2},{2,3},{3,4},{4,5},{5,6},{6,7},{7,8},{8,9},{9,10},{10,1... | collective-permute-start | bytes 196616 | tf_op jit(solution)/shard_map/ppermute | solution.py:17
  619.9 8.1 %collective-permute-start.4 = (f32[64,2,128]{2,0,1:T(8,128)S(1)}, f32[64,2,128]{2,0,1:T(8,128)S(1)}, u32[]{:S(2)}, u32[]{:S(2)}) collective-permute-start(f32[64,2,128]{2,0,1:T(8,128)S(1)} %get-tuple-element.246), channel_id=1, source_target_pairs={{0,2},{1,3},{2,4},{3,5},{4,6},{5,7},{6,8},{7,9},{8,10},{9,11},{10,... | collective-permute-start | bytes 196616 | tf_op jit(solution)/shard_map/ppermute | solution.py:17
  621.8 11.0 %collective-permute-start.5 = (f32[64,2,128]{2,0,1:T(8,128)S(1)}, f32[64,2,128]{2,0,1:T(8,128)S(1)}, u32[]{:S(2)}, u32[]{:S(2)}) collective-permute-start(f32[64,2,128]{2,0,1:T(8,128)S(1)} %get-tuple-element.245), channel_id=1, source_target_pairs={{0,3},{1,4},{2,5},{3,6},{4,7},{5,8},{6,9},{7,10},{8,11},{9,12},{10... | collective-permute-start | bytes 196616 | tf_op jit(solution)/shard_map/ppermute | solution.py:17
where the time goes:
time: 640 us; the launch traced here: 633 us
  waiting for transfers between devices  192 us (30%)
  loops' own time  157 us (25%)
  local copies, waits for them, and re-layouts  126 us (20%)
  other arithmetic  68.7 us (11%)
  matrix products  35.3 us (6%)
  starting transfers between devices  28 us (4%)
  blocking collectives  25.7 us (4%)
    ppermute x6, waiting for transfers between devices, shifted(): return lax.ppermute(value, axis, pairs)  192 us
    another operation x16, loops' own time, coherence_sums(): lax.map(one_piece, jnp.arange(freq_count // piece_bins) * piece_bins)  125 us
    dynamic_slice x64, local copies, waits for them, and re-layouts, coherence_sums(): lax.map(one_piece, jnp.arange(freq_count // piece_bins) * piece_bins)  41.9 us
    reduce_sum x64, other arithmetic, one_piece(): return (jnp.sum(modulus, axis=2), jnp.sum(modulus, axis=1))  33.9 us
    dynamic_slice x32, local copies, waits for them, and re-layouts, visit(): left_block = lax.dynamic_index_in_dim(blocks, left_index, 3, keepdims=False)  32.7 us
    another operation x1, loops' own time, body(): totals = lax.fori_loop(0, pair_blocks.shape[0], visit, start_totals)  32.5 us
    dot_general x64, matrix products, one_piece(): jnp.einsum('kfi,pkfj->pfij', left_piece, right_piece, preferred_element_t...  31.1 us
    ppermute x6, starting transfers between devices, shifted(): return lax.ppermute(value, axis, pairs)  28 us
  transfers between devices with their start and end apart: 6, of which 5 were waited for; matrix products, arithmetic and copies ran while one was open for 1% of the time, Pallas kernels for 0%

commit v1 on v0

v1 whole, which is shorter than its diff:
```python
import functools

import jax
import jax.numpy as jnp
from jax import lax
from jax.experimental import pallas as pl
from jax.experimental.pallas import tpu as pltpu
from jax.sharding import PartitionSpec as P

MESH = pl.DeviceIdType.MESH
SB = 128
HALF = 64
EPS = 1e-06
TINY = 1.1754944e-38
FQ = 8
OWN = 64
WIN = 24
W_DEV = 3
FREQ = 512
F_DEV = 64
ST = 256
T = 4
F_PART = F_DEV // T
F_HALF = F_PART // 2
KDIM = 2 * WIN
UNROLL = 4


def modulus(square):
    return square * lax.rsqrt(jnp.maximum(square, TINY))


def whiten(spec, white):
    @pl.loop(0, W_DEV)
    def _(w):
        re = spec[0, w].astype(jnp.float32)
        im = spec[1, w].astype(jnp.float32)
        mag = modulus(re * re + im * im)
        high = mag.astype(jnp.bfloat16)
        rest = mag - high.astype(jnp.float32)
        mid = rest.astype(jnp.bfloat16)
        low = (rest - mid.astype(jnp.float32)).astype(jnp.bfloat16)
        for tile in range(FREQ // 128):
            first = tile * 128
            start = min(max(first - HALF, 0), FREQ - 256)
            out_bin = lax.broadcasted_iota(jnp.int32, (128, 256), 0) + first
            in_bin = lax.broadcasted_iota(jnp.int32, (128, 256), 1) + start
            band = jnp.where(jnp.abs(out_bin - in_bin) <= HALF, 1.0, 0.0).astype(jnp.bfloat16)
            rows = slice(start, start + 256)
            total = jnp.dot(band, low[rows], preferred_element_type=jnp.float32)
            total += jnp.dot(band, mid[rows], preferred_element_type=jnp.float32)
            total += jnp.dot(band, high[rows], preferred_element_type=jnp.float32)
            bins = lax.broadcasted_iota(jnp.int32, (128, ST), 0) + first
            counted = jnp.minimum(bins + HALF, FREQ - 1) - jnp.maximum(bins - HALF, 0) + 1
            inverse = 1.0 / (total / counted.astype(jnp.float32) + EPS)
            here = slice(first, first + 128)
            white[0, w, here] = (re[here] * inverse).astype(jnp.bfloat16)
            white[1, w, here] = (im[here] * inverse).astype(jnp.bfloat16)


def one_bin(anchor, partners, weight, f):
    first = anchor[f]
    wide = first.astype(jnp.float32)
    turned = jnp.concatenate([wide[WIN:], -wide[:WIN]], axis=0).astype(jnp.bfloat16)
    left = jnp.concatenate([first, turned], axis=1).T
    right = [partner[f] for partner in partners]
    cols = [None] * 8
    rows = []
    for p in range(2):
        pieces = []
        for i in range(2):
            at = p * SB + i * 64
            lhs = jnp.concatenate([left[at : at + 64], left[ST + at : ST + at + 64]], axis=0)
            piece = None
            for s in range(4):
                cross = jnp.dot(lhs, right[s], preferred_element_type=jnp.float32)
                for h in range(2):
                    q = 2 * s + h
                    if not p <= q <= p + 6:
                        continue
                    lanes = slice(h * SB, (h + 1) * SB)
                    re, im = cross[:64, lanes], cross[64:, lanes]
                    value = modulus(re * re + im * im) * weight(p, q)
                    col = jnp.sum(value.reshape(8, 8, SB), axis=0)
                    cols[q] = col if cols[q] is None else cols[q] + col
                    piece = value if piece is None else piece + value
            pieces.append(piece)
        across = jnp.concatenate(pieces, axis=0).T
        rows.append(jnp.sum(across.reshape(16, 8, SB), axis=0).sum(axis=0, keepdims=True))
    return rows, [col.sum(axis=0, keepdims=True) for col in cols]


def eight_bins(anchor_slot, partners, weight, start, out):
    line = lax.broadcasted_iota(jnp.int32, (8, SB), 0)

    def step(k, tiles):
        rows, cols = one_bin(partners[anchor_slot], partners, weight, start + k)
        for p in range(2):
            cols[2 * anchor_slot + p] = cols[2 * anchor_slot + p] + rows[p]
        return tuple(jnp.where(line == k, cols[q], tiles[q]) for q in range(8))

    zero = jnp.zeros((8, SB), jnp.float32)
    tiles = lax.fori_loop(0, 8, step, (zero,) * 8, unroll=UNROLL)
    for q in range(8):
        out[q // 2, pl.ds(start, 8), (q % 2) * SB : (q % 2 + 1) * SB] = tiles[q]


def kernel(
    spec, blocks, valid, out,
    white, landed, wide, held, left, right, far, counts, sums, back,
    a2a_send, a2a_recv, hop_send, hop_recv, far_send, far_recv,
    cnt_send, cnt_recv, ret_send, ret_recv,
):
    me = lax.axis_index("freq")
    owner = lax.axis_index("pair")

    def along(by):
        return (me, lax.rem(owner + by + OWN, OWN))

    barrier = pltpu.get_barrier_semaphore()
    for by in range(1, FQ):
        pl.semaphore_signal(barrier, 1, device_id=(lax.rem(me + by, FQ), owner), device_id_type=MESH)
    for by in (-2, -1, 1, 2):
        pl.semaphore_signal(barrier, 1, device_id=along(by), device_id_type=MESH)

    row = lax.broadcasted_iota(jnp.int32, (16, SB), 0)
    table = jnp.zeros((16, SB), jnp.float32)
    for slot in range(16):
        first = blocks[slot, 0] - 2 * owner
        second = blocks[slot, 1] - 2 * owner
        table += jnp.where(row == first * 8 + second, valid[slot].astype(jnp.float32), 0.0)
    counts[2] = table * (1.0 / (WIN * SB))

    whiten(spec, white)
    mine = pl.multiple_of(me * F_DEV, F_DEV)
    landed[me] = white[:, :, pl.ds(mine, F_DEV), :]
    pl.semaphore_wait(barrier, FQ - 1 + 4)

    def copy(src, dst, send, recv, device):
        return pltpu.make_async_remote_copy(
            src_ref=src, dst_ref=dst, send_sem=send, recv_sem=recv, device_id=device, device_id_type=MESH
        )

    def regroup(by, t):
        peer = lax.rem(me + by, FQ)
        bins = pl.ds(pl.multiple_of(peer * F_DEV + t * F_PART, F_PART), F_PART)
        return copy(
            white.at[:, :, bins, :],
            landed.at[me, :, :, pl.ds(pl.multiple_of(t * F_PART, F_PART), F_PART), :],
            a2a_send.at[by - 1, t], a2a_recv.at[by - 1, t], (peer, owner),
        )

    def count_copies():
        return [
            copy(counts.at[2], counts.at[to], cnt_send.at[i], cnt_recv.at[i], along(by))
            for i, (to, by) in enumerate(((1, 1), (0, 2), (3, -1)))
        ]

    def hop(side, t, part):
        bins = pl.ds(t * F_PART + part * F_HALF, F_HALF)
        dst, by = ((right, -1), (left, 1))[side]
        at = 2 * t + part
        return copy(held.at[bins], dst.at[bins], hop_send.at[side, at], hop_recv.at[side, at], along(by))

    def relay(part, t):
        bins = pl.ds(t * F_PART + part * F_HALF, F_HALF)
        src, by = ((right, -1), (left, 1))[part]
        at = 2 * t + part
        return copy(src.at[bins], far.at[bins], far_send.at[at], far_recv.at[at], along(by))

    def returned(part, t):
        at = 2 * t + part
        bins = pl.ds(pl.multiple_of(at * F_HALF, F_HALF), F_HALF)
        plan = (((0, -1, 0), (2, 1, 1), (3, 2, 2)), ((1, -1, 0), (3, 1, 1), (0, -2, 2)))[part]
        return [
            copy(sums.at[slot, bins, :], back.at[to, bins, :], ret_send.at[to, at], ret_recv.at[to, at], along(by))
            for slot, by, to in plan
        ]

    def arrange(t):
        for by in range(1, FQ):
            regroup(by, t).wait_recv()
        bins = pl.ds(pl.multiple_of(t * F_PART, F_PART), F_PART)
        for source in range(FQ):
            for c in range(2):
                for w in range(W_DEV):
                    k = c * WIN + source * W_DEV + w
                    value = landed[source, c, w, bins, :].astype(jnp.float32)
                    for h in range(2):
                        wide[h, k * F_PART : (k + 1) * F_PART, :] = value[:, h * SB : (h + 1) * SB]
        for f in range(F_PART):
            for h in range(2):
                value = wide[h, pl.ds(f, KDIM, stride=F_PART), :]
                held[t * F_PART + f, :, h * SB : (h + 1) * SB] = value.astype(jnp.bfloat16)
        for side, part in ((0, 0), (1, 1), (0, 1), (1, 0)):
            hop(side, t, part).start()

    def pass_on(t):
        hop(0, t, 0).wait_recv()
        relay(0, t).start()
        hop(1, t, 1).wait_recv()
        relay(1, t).start()

    def compute(t):
        hop(1, t, 0).wait_recv()
        relay(0, t).wait_recv()
        start = pl.multiple_of(t * F_PART, F_HALF)
        eight_bins(0, (left, held, right, far), lambda p, q: counts[1, p * 8 + q : p * 8 + q + 1, :], start, sums)
        for item in returned(0, t):
            item.start()
        hop(0, t, 1).wait_recv()
        relay(1, t).wait_recv()
        start = pl.multiple_of(t * F_PART + F_HALF, F_HALF)

        def weight(p, q):
            at = (q % 2) * 8 + 6 - 2 * (q // 2) + p
            return counts[q // 2, at : at + 1, :]

        eight_bins(3, (far, left, held, right), weight, start, sums)
        for item in returned(1, t):
            item.start()

    for t in range(T):
        for by in range(1, FQ):
            regroup(by, t).start()
    for item in count_copies():
        item.start()
    arrange(0)
    for item in count_copies():
        item.wait_recv()

    @pl.loop(0, T + 1)
    def _(t):
        @pl.when(t < T - 1)
        def _():
            arrange(t + 1)

        @pl.when(t < T)
        def _():
            pass_on(t)

        @pl.when(t > 0)
        def _():
            compute(t - 1)

    for t in range(T):
        for part in range(2):
            for item in returned(part, t):
                item.wait_recv()
            bins = slice((2 * t + part) * F_HALF, (2 * t + part + 1) * F_HALF)
            out[bins] = (sums[1 + part, bins] + back[0, bins]) + (back[1, bins] + back[2, bins])
    for t in range(T):
        for by in range(1, FQ):
            regroup(by, t).wait_send()
        for part in range(2):
            for side in range(2):
                hop(side, t, part).wait_send()
            relay(part, t).wait_send()
            for item in returned(part, t):
                item.wait_send()
    for item in count_copies():
        item.wait_send()


def body(spectra, pair_blocks, pair_valid):
    dma = pltpu.SemaphoreType.DMA
    band = pltpu.VMEM((F_DEV, KDIM, ST), jnp.bfloat16)
    vmem = pl.BlockSpec(memory_space=pltpu.VMEM)
    smem = pl.BlockSpec(memory_space=pltpu.SMEM)
    return pl.pallas_call(
        kernel,
        out_shape=jax.ShapeDtypeStruct((F_DEV, ST), jnp.float32),
        in_specs=[vmem, smem, smem],
        out_specs=vmem,
        scratch_shapes=[
            pltpu.VMEM((2, W_DEV, FREQ, ST), jnp.bfloat16),
            pltpu.VMEM((FQ, 2, W_DEV, F_DEV, ST), jnp.bfloat16),
            pltpu.VMEM((2, KDIM * F_PART, SB), jnp.float32),
            band, band, band, band,
            pltpu.VMEM((4, 16, SB), jnp.float32),
            pltpu.VMEM((4, F_DEV, ST), jnp.float32),
            pltpu.VMEM((3, F_DEV, ST), jnp.float32),
            dma((FQ - 1, T)), dma((FQ - 1, T)),
            dma((2, 2 * T)), dma((2, 2 * T)),
            dma((2 * T,)), dma((2 * T,)),
            dma((3,)), dma((3,)),
            dma((3, 2 * T)), dma((3, 2 * T)),
        ],
        compiler_params=pltpu.CompilerParams(
            collective_id=0, has_side_effects=True, vmem_limit_bytes=40 * 2**20
        ),
        cost_estimate=pl.CostEstimate(flops=8 * 10**9, bytes_accessed=2 * 2**20, transcendentals=0),
    )(spectra, pair_blocks, pair_valid)


def solution(mesh):
    in_specs = (P(None, "freq", None, "pair"), P("pair", None), P("pair"))
    out_specs = P("freq", "pair")
    return jax.shard_map(body, mesh=mesh, in_specs=in_specs, out_specs=out_specs, check_vma=False)
```

time: 640 us -> 94.9 us (0.15)
  the two profiles are of different devices: /device:TPU:7 before, /device:TPU:1 now
where the time goes in v1:
time: 94.9 us; the launch traced here: 94.7 us
  Pallas kernels  91.3 us (96%)
  local copies, waits for them, and re-layouts  3.45 us (4%)
    pallas_call x1, Pallas kernels, body(): pl.pallas_call(kernel, out_shape=jax.ShapeDtypeStruct((F_DEV, ST), jnp.fl...  91.3 us
    unnamed x6, local copies, waits for them, and re-layouts  3.45 us

profile of v1, /device:TPU:1, one launch (start us, length us, event | category | flops | bytes accessed | tf_op | source)
XLA Modules:
  0.0 94.7 jit_solution(11721931614353905364)
XLA Ops:
  0.0 0.8 copy.4.blocks
  0.8 0.0 copy-start
  0.8 1.4 %copy-done = bf16[2,3,512,256]{3,2,1,0:T(8,128)(2,1)S(1)} copy-done((bf16[2,3,512,256]{3,2,1,0:T(8,128)(2,1)S(1)}, bf16[2,3,512,256]{3,2,1,0:T(8,128)(2,1)}, u32[]{:S(2)}) %copy-start) | copy-done | bytes 1572888
  2.2 0.0 copy-start.1
  2.2 0.7 copy-done.1
  2.8 91.3 %shard_map.37 = f32[64,256]{1,0:T(8,128)S(1)} custom-call(bf16[2,3,512,256]{3,2,1,0:T(8,128)(2,1)S(1)} %copy-done, s32[16,2]{1,0:T(8,128)S(1)} %copy.4.blocks, s32[16]{0:T(128)S(1)} %copy-done.1), custom_call_target="tpu_custom_call" | custom-call | flops 8000000000 | bytes 2097152 | tf_op jit(solution)/shard_map/pallas_call | solution.py:270
  94.1 0.6 copy.6
Async XLA Ops:
  0.8 1.4 %copy-start = (bf16[2,3,512,256]{3,2,1,0:T(8,128)(2,1)S(1)}, bf16[2,3,512,256]{3,2,1,0:T(8,128)(2,1)}, u32[]{:S(2)}) copy-start(bf16[2,3,512,256]{3,2,1,0:T(8,128)(2,1)} %spec.1) | copy-start | bytes 4718596
  2.2 0.7 copy-start.1

commit v2 on v1

v2 whole, which is shorter than its diff:
```python
import functools

import jax
import jax.numpy as jnp
from jax import lax
from jax.experimental import pallas as pl
from jax.experimental.pallas import tpu as pltpu
from jax.sharding import PartitionSpec as P

MESH = pl.DeviceIdType.MESH
SB = 128
HALF = 64
EPS = 1e-06
TINY = 1.1754944e-38
FQ = 8
OWN = 64
WIN = 24
W_DEV = 3
FREQ = 512
F_DEV = 64
ST = 256
T = 4
F_PART = F_DEV // T
F_HALF = F_PART // 2
KDIM = 2 * WIN
UNROLL = 4
LAST = (0, 0, 1, 1, 0, 1, 0, 1)


def modulus(square):
    return square * lax.rsqrt(jnp.maximum(square, TINY))


def whiten(spec, white, first_window, windows):
    @pl.loop(first_window, first_window + windows)
    def _(w):
        re = spec[0, w].astype(jnp.float32)
        im = spec[1, w].astype(jnp.float32)
        mag = modulus(re * re + im * im)
        high = mag.astype(jnp.bfloat16)
        rest = mag - high.astype(jnp.float32)
        mid = rest.astype(jnp.bfloat16)
        low = (rest - mid.astype(jnp.float32)).astype(jnp.bfloat16)
        for tile in range(FREQ // 128):
            first = tile * 128
            start = min(max(first - HALF, 0), FREQ - 256)
            out_bin = lax.broadcasted_iota(jnp.int32, (128, 256), 0) + first
            in_bin = lax.broadcasted_iota(jnp.int32, (128, 256), 1) + start
            band = jnp.where(jnp.abs(out_bin - in_bin) <= HALF, 1.0, 0.0).astype(jnp.bfloat16)
            rows = slice(start, start + 256)
            total = jnp.dot(band, low[rows], preferred_element_type=jnp.float32)
            total += jnp.dot(band, mid[rows], preferred_element_type=jnp.float32)
            total += jnp.dot(band, high[rows], preferred_element_type=jnp.float32)
            bins = lax.broadcasted_iota(jnp.int32, (128, ST), 0) + first
            counted = jnp.minimum(bins + HALF, FREQ - 1) - jnp.maximum(bins - HALF, 0) + 1
            inverse = 1.0 / (total / counted.astype(jnp.float32) + EPS)
            here = slice(first, first + 128)
            two = slice(first // F_DEV, first // F_DEV + 2)
            white[0, w, two] = (re[here] * inverse).astype(jnp.bfloat16).reshape(2, F_DEV, ST)
            white[1, w, two] = (im[here] * inverse).astype(jnp.bfloat16).reshape(2, F_DEV, ST)


def one_bin(anchor, partners, weight, f):
    first = anchor[f]
    wide = first.astype(jnp.float32)
    turned = jnp.concatenate([wide[WIN:], -wide[:WIN]], axis=0).astype(jnp.bfloat16)
    left = jnp.concatenate([first, turned], axis=1).T
    right = {s: partner[f] for s, partner in partners.items()}
    cols = {}
    rows = []
    for p in range(2):
        pieces = []
        for i in range(2):
            at = p * SB + i * 64
            lhs = jnp.concatenate([left[at : at + 64], left[ST + at : ST + at + 64]], axis=0)
            piece = None
            for s in partners:
                cross = jnp.dot(lhs, right[s], preferred_element_type=jnp.float32)
                for h in range(2):
                    q = 2 * s + h
                    if not p <= q <= p + 6:
                        continue
                    lanes = slice(h * SB, (h + 1) * SB)
                    re, im = cross[:64, lanes], cross[64:, lanes]
                    value = modulus(re * re + im * im) * weight(p, q)
                    col = jnp.sum(value.reshape(8, 8, SB), axis=0)
                    cols[q] = cols[q] + col if q in cols else col
                    piece = value if piece is None else piece + value
            pieces.append(piece)
        across = jnp.concatenate(pieces, axis=0).T
        rows.append(jnp.sum(across.reshape(16, 8, SB), axis=0).sum(axis=0, keepdims=True))
    return rows, {q: col.sum(axis=0, keepdims=True) for q, col in cols.items()}


def eight_bins(anchor_slot, anchor, partners, weight, start, out):
    line = lax.broadcasted_iota(jnp.int32, (8, SB), 0)
    near = anchor_slot in partners
    own = [2 * anchor_slot, 2 * anchor_slot + 1]
    keys = sorted({2 * s + h for s in partners for h in range(2)} | set(own))

    def step(k, tiles):
        rows, cols = one_bin(anchor, partners, weight, start + k)
        for p in range(2):
            cols[own[p]] = cols[own[p]] + rows[p] if near else rows[p]
        return tuple(jnp.where(line == k, cols[q], tile) for q, tile in zip(keys, tiles))

    zero = jnp.zeros((8, SB), jnp.float32)
    tiles = lax.fori_loop(0, 8, step, (zero,) * len(keys), unroll=UNROLL)
    for q, tile in zip(keys, tiles):
        place = (q // 2, pl.ds(start, 8), slice((q % 2) * SB, (q % 2 + 1) * SB))
        out[place] = tile if near or q not in own else out[place] + tile


def kernel(
    spec_hbm, blocks_hbm, valid_hbm, out,
    spec, blocks, valid, load_sem, white, from_left, from_right, from_far, landed, more, wide,
    held, left, right, far, counts, sums, back,
    a2a_send, a2a_recv, more_send, more_recv, hop_send, hop_recv, far_send, far_recv,
    cnt_send, cnt_recv, ret_send, ret_recv, early_send, early_recv, ready,
):
    me = lax.axis_index("freq")
    owner = lax.axis_index("pair")

    def along(by):
        return (me, lax.rem(owner + by + OWN, OWN))

    def signal(sem, device):
        pl.semaphore_signal(sem, 1, device_id=device, device_id_type=MESH)

    barrier = pltpu.get_barrier_semaphore()
    for by in (-1, 1):
        signal(barrier, along(by))
    for by in range(1, FQ):
        signal(barrier, (lax.rem(me + by, FQ), owner))

    loads = [pltpu.make_async_copy(spec_hbm.at[:, w], spec.at[:, w], load_sem.at[w]) for w in range(W_DEV)]
    loads.append(pltpu.make_async_copy(blocks_hbm, blocks, load_sem.at[W_DEV]))
    loads.append(pltpu.make_async_copy(valid_hbm, valid, load_sem.at[W_DEV + 1]))
    for load in loads:
        load.start()
    loads[W_DEV].wait()
    loads[W_DEV + 1].wait()
    row = lax.broadcasted_iota(jnp.int32, (16, 16), 0)
    place = (blocks[0:1, :] - 2 * owner) * 8 + (blocks[1:2, :] - 2 * owner)
    table = jnp.sum(jnp.where(row == place, valid[...].astype(jnp.float32), 0.0), axis=1, keepdims=True)
    counts[2] = jnp.broadcast_to(table * (1.0 / (WIN * SB)), (16, SB))

    def copy(src, dst, send, recv, device):
        return pltpu.make_async_remote_copy(
            src_ref=src, dst_ref=dst, send_sem=send, recv_sem=recv, device_id=device, device_id_type=MESH
        )

    def early(side, w):
        dst, by = ((from_right, -1), (from_left, 1))[side]
        return copy(
            white.at[:, w, :, pl.ds(0, F_PART), :], dst.at[:, w],
            early_send.at[side, w], early_recv.at[side, w], along(by),
        )

    def early_relay(w):
        return copy(
            from_right.at[:, w], from_far.at[:, w], early_send.at[2, w], early_recv.at[2, w], along(-1)
        )

    def regroup_more(i, by):
        peer = lax.rem(me + by, FQ)
        src = (from_left, from_right, from_far)[i]
        return copy(
            src.at[:, :, peer, :, :], more.at[i, by - 1],
            more_send.at[i, by - 1], more_recv.at[i, by - 1], (peer, owner),
        )

    def part_bins(t):
        return pl.ds(pl.multiple_of(t * F_PART, F_PART), F_PART)

    def regroup(by, t):
        peer = lax.rem(me + by, FQ)
        return copy(
            white.at[:, :, peer, part_bins(t), :], landed.at[by - 1, :, :, part_bins(t), :],
            a2a_send.at[by - 1, t], a2a_recv.at[by - 1, t], (peer, owner),
        )

    def count_copies():
        return [
            copy(counts.at[2], counts.at[to], cnt_send.at[i], cnt_recv.at[i], along(by))
            for i, (to, by) in enumerate(((1, 1), (3, -1), (0, 2)))
        ]

    def hop(side, t, part):
        bins = pl.ds(t * F_PART + part * F_HALF, F_HALF)
        dst, by = ((right, -1), (left, 1))[side]
        at = 2 * t + part
        return copy(held.at[bins], dst.at[bins], hop_send.at[side, at], hop_recv.at[side, at], along(by))

    def relay(last, t, part):
        bins = pl.ds(t * F_PART + part * F_HALF, F_HALF)
        src, by = ((right, -1), (left, 1))[last]
        at = 2 * t + part
        return copy(src.at[bins], far.at[bins], far_send.at[at], far_recv.at[at], along(by))

    def returned(last, at, stage):
        bins = pl.ds(pl.multiple_of(at * F_HALF, F_HALF), F_HALF)
        plan = ((((2, 1, 1),), ((0, -1, 0), (3, 2, 2))), (((1, -1, 0),), ((3, 1, 1), (0, -2, 2))))[last][stage]
        return [
            copy(sums.at[slot, bins, :], back.at[to, bins, :], ret_send.at[to, at], ret_recv.at[to, at], along(by))
            for slot, by, to in plan
        ]

    def place_part(dst, t, first, others, arrived):
        for by in range(FQ):
            if by:
                arrived(by)
            for c in range(2):
                for w in range(W_DEV):
                    k = c * WIN + by * W_DEV + w
                    value = (others(by, c, w) if by else first(c, w)).astype(jnp.float32)
                    for h in range(2):
                        wide[h, k * F_PART : (k + 1) * F_PART, :] = value[:, h * SB : (h + 1) * SB]
        for f in range(F_PART):
            for h in range(2):
                value = wide[h, pl.ds(f, KDIM, stride=F_PART), :]
                dst[t * F_PART + f, :, h * SB : (h + 1) * SB] = value.astype(jnp.bfloat16)

    def arrange(t):
        bins = part_bins(t)
        place_part(
            held, t, lambda c, w: white[c, w, me, bins, :], lambda by, c, w: landed[by - 1, c, w, bins, :],
            lambda by: regroup(by, t).wait_recv(),
        )

    def arrange_more(i):
        src = (from_left, from_right, from_far)[i]
        place_part(
            (left, right, far)[i], 0, lambda c, w: src[c, w, me], lambda by, c, w: more[i, by - 1, c, w],
            lambda by: regroup_more(i, by).wait_recv(),
        )

    def start_hops(t):
        for side, part in ((0, 0), (1, 1), (0, 1), (1, 0)):
            hop(side, t, part).start()

    def pass_on(t):
        hop(0, t, 0).wait_recv()
        relay(0, t, 0).start()
        hop(1, t, 1).wait_recv()
        relay(1, t, 1).start()

    def weight_first(p, q):
        return counts[1, p * 8 + q : p * 8 + q + 1, :]

    def weight_last(p, q):
        at = (q % 2) * 8 + 6 - 2 * (q // 2) + p
        return counts[q // 2, at : at + 1, :]

    def compute(last, at, stage):
        start = pl.multiple_of(at * F_HALF, F_HALF)
        if last:
            partners = {0: far} if stage else {1: left, 2: held, 3: right}
            eight_bins(3, right, partners, weight_last, start, sums)
        else:
            partners = {3: far} if stage else {0: left, 1: held, 2: right}
            eight_bins(0, left, partners, weight_first, start, sums)
        for item in returned(last, at, stage):
            item.start()

    for w in range(W_DEV):
        loads[w].wait()
        whiten(spec, white, w, 1)
        if w == 0:
            pl.semaphore_wait(barrier, FQ - 1 + 2)
            signal(ready.at[0], along(1))
            signal(ready.at[1], along(-1))
        early(0, w).start()
        early(1, w).start()
    for t in (1, 2, 3, 0):
        for by in range(1, FQ):
            regroup(by, t).start()
    for item in count_copies()[:2]:
        item.start()
    arrange(1)
    start_hops(1)
    for w in range(W_DEV):
        early(0, w).wait_recv()
        early(1, w).wait_recv()
    for i in range(2):
        for by in range(1, FQ):
            regroup_more(i, by).start()
    pl.semaphore_wait(ready.at[0], 1)
    pl.semaphore_wait(ready.at[1], 1)
    count_copies()[2].start()

    @pl.loop(2, T)
    def _(t):
        arrange(t)
        start_hops(t)

    for w in range(W_DEV):
        early_relay(w).start()
    for part in range(2):
        hop(1, 1, part).wait_recv()
        relay(1, 1, part).start()
    for item in count_copies():
        item.wait_recv()
    hop(0, 1, 0).wait_recv()
    hop(0, 1, 1).wait_recv()

    @pl.loop(2, 4)
    def _(at):
        compute(1, at, 0)

    arrange(0)
    arrange_more(0)
    arrange_more(1)

    @pl.loop(0, 2)
    def _(at):
        compute(0, at, 0)

    @pl.loop(2, T)
    def _(t):
        pass_on(t)
        hop(1, t, 0).wait_recv()
        hop(0, t, 1).wait_recv()
        compute(0, 2 * t, 0)
        compute(1, 2 * t + 1, 0)

    for w in range(W_DEV):
        early_relay(w).wait_recv()
    for by in range(1, FQ):
        regroup_more(2, by).start()

    @pl.loop(2, 4)
    def _(at):
        relay(1, 1, at - 2).wait_recv()
        compute(1, at, 1)

    @pl.loop(2, T)
    def _(t):
        relay(0, t, 0).wait_recv()
        compute(0, 2 * t, 1)
        relay(1, t, 1).wait_recv()
        compute(1, 2 * t + 1, 1)

        @pl.when(t == 2)
        def _():
            arrange_more(2)

            @pl.loop(0, 2)
            def _(at):
                compute(0, at, 1)

    for at in range(2 * T):
        last = LAST[at]
        for item in returned(last, at, 0) + returned(last, at, 1):
            item.wait_recv()
        bins = slice(at * F_HALF, (at + 1) * F_HALF)
        out[bins] = (sums[1 + last, bins] + back[0, bins]) + (back[1, bins] + back[2, bins])
    for t in range(T):
        for by in range(1, FQ):
            regroup(by, t).wait_send()
        for part in range(2):
            at = 2 * t + part
            last = LAST[at]
            if t:
                hop(0, t, part).wait_send()
                hop(1, t, part).wait_send()
                relay(last, t, part).wait_send()
            for item in returned(last, at, 0) + returned(last, at, 1):
                item.wait_send()
    for w in range(W_DEV):
        early(0, w).wait_send()
        early(1, w).wait_send()
        early_relay(w).wait_send()
    for i in range(3):
        for by in range(1, FQ):
            regroup_more(i, by).wait_send()
    for item in count_copies():
        item.wait_send()


def body(spectra, pair_blocks, pair_valid):
    dma = pltpu.SemaphoreType.DMA
    band = pltpu.VMEM((F_DEV, KDIM, ST), jnp.bfloat16)
    early = pltpu.VMEM((2, W_DEV, FQ, F_PART, ST), jnp.bfloat16)
    vmem = pl.BlockSpec(memory_space=pltpu.VMEM)
    anywhere = pl.BlockSpec(memory_space=pl.ANY)
    return pl.pallas_call(
        kernel,
        out_shape=jax.ShapeDtypeStruct((F_DEV, ST), jnp.float32),
        in_specs=[anywhere, anywhere, anywhere],
        out_specs=vmem,
        scratch_shapes=[
            pltpu.VMEM((2, W_DEV, FREQ, ST), jnp.bfloat16),
            pltpu.VMEM((2, 16), jnp.int32),
            pltpu.VMEM((1, 16), jnp.int32),
            dma((W_DEV + 2,)),
            pltpu.VMEM((2, W_DEV, FQ, F_DEV, ST), jnp.bfloat16),
            early, early, early,
            pltpu.VMEM((FQ - 1, 2, W_DEV, F_DEV, ST), jnp.bfloat16),
            pltpu.VMEM((3, FQ - 1, 2, W_DEV, F_PART, ST), jnp.bfloat16),
            pltpu.VMEM((2, KDIM * F_PART, SB), jnp.float32),
            band, band, band, band,
            pltpu.VMEM((4, 16, SB), jnp.float32),
            pltpu.VMEM((4, F_DEV, ST), jnp.float32),
            pltpu.VMEM((3, F_DEV, ST), jnp.float32),
            dma((FQ - 1, T)), dma((FQ - 1, T)),
            dma((3, FQ - 1)), dma((3, FQ - 1)),
            dma((2, 2 * T)), dma((2, 2 * T)),
            dma((2 * T,)), dma((2 * T,)),
            dma((3,)), dma((3,)),
            dma((3, 2 * T)), dma((3, 2 * T)),
            dma((3, W_DEV)), dma((3, W_DEV)),
            pltpu.SemaphoreType.REGULAR((2,)),
        ],
        compiler_params=pltpu.CompilerParams(
            collective_id=0, has_side_effects=True, vmem_limit_bytes=60 * 2**20
        ),
        cost_estimate=pl.CostEstimate(flops=8 * 10**9, bytes_accessed=2 * 2**20, transcendentals=0),
    )(spectra, pair_blocks.T, pair_valid.reshape(1, 16))


def solution(mesh):
    in_specs = (P(None, "freq", None, "pair"), P("pair", None), P("pair"))
    out_specs = P("freq", "pair")
    return jax.shard_map(body, mesh=mesh, in_specs=in_specs, out_specs=out_specs, check_vma=False)
```

time: 94.9 us -> 81.2 us (0.86)
  Pallas kernels: 91.3 us -> 79.5 us
  local copies, waits for them, and re-layouts: 3.45 us -> 1.47 us
    pallas_call x1, Pallas kernels: 91.3 us -> 79.5 us  [body(): pl.pallas_call(kernel, out_shape=jax.ShapeDtypeStruct((F_DEV, ST), jnp.fl...]
    unnamed x6 -> x1, local copies, waits for them, and re-layouts: 3.45 us -> 1.47 us
where the time goes in v2:
time: 81.2 us; the launch traced here: 81 us
  Pallas kernels  79.5 us (98%)
  local copies, waits for them, and re-layouts  1.47 us (2%)
    pallas_call x1, Pallas kernels, body(): pl.pallas_call(kernel, out_shape=jax.ShapeDtypeStruct((F_DEV, ST), jnp.fl...  79.5 us

profile of v2, /device:TPU:1, one launch (start us, length us, event | category | flops | bytes accessed | tf_op | source)
XLA Modules:
  0.0 81.0 jit_solution(2223715679835821722)
XLA Ops:
  0.0 79.5 %shard_map.37 = f32[64,256]{1,0:T(8,128)} custom-call(bf16[2,3,512,256]{3,2,1,0:T(8,128)(2,1)} %spec_hbm.1, s32[2,16]{1,0:T(2,128)} %bitcast.2, s32[1,16]{1,0:T(1,128)} %bitcast.3), custom_call_target="tpu_custom_call" | custom-call | flops 8000000000 | bytes 2097152 | tf_op jit(solution)/shard_map/pallas_call | solution.py:387
  79.5 1.5 %copy.5 = f32[64,256]{1,0:T(8,128)} copy(f32[64,256]{1,0:T(8,128)} %shard_map.37) | data formatting | bytes 131072

commit v3 on v2

--- a/solution.py
+++ b/solution.py
@@ -105,22 +105,45 @@
         return tuple(jnp.where(line == k, cols[q], tile) for q, tile in zip(keys, tiles))
 
     zero = jnp.zeros((8, SB), jnp.float32)
-    tiles = lax.fori_loop(0, 8, step, (zero,) * len(keys), unroll=UNROLL)
+    tiles = lax.fori_loop(0, 8, step, (zero,) * len(keys), unroll=UNROLL if len(partners) > 1 else 8)
     for q, tile in zip(keys, tiles):
         place = (q // 2, pl.ds(start, 8), slice((q % 2) * SB, (q % 2 + 1) * SB))
         out[place] = tile if near or q not in own else out[place] + tile
 
 
+class Guarded:
+    def __init__(self, copy, sends, receives):
+        self.copy, self.sends, self.receives = copy, sends, receives
+
+    def start(self):
+        @pl.when(self.sends)
+        def _():
+            self.copy.start()
+
+    def wait_send(self):
+        @pl.when(self.sends)
+        def _():
+            self.copy.wait_send()
+
+    def wait_recv(self):
+        @pl.when(self.receives)
+        def _():
+            self.copy.wait_recv()
+
+
 def kernel(
     spec_hbm, blocks_hbm, valid_hbm, out,
     spec, blocks, valid, load_sem, white, from_left, from_right, from_far, landed, more, wide,
-    held, left, right, far, counts, sums, back,
+    held, left, right, far, counts, sums, back, own,
     a2a_send, a2a_recv, more_send, more_recv, hop_send, hop_recv, far_send, far_recv,
     cnt_send, cnt_recv, ret_send, ret_recv, early_send, early_recv, ready,
 ):
     me = lax.axis_index("freq")
     owner = lax.axis_index("pair")
 
+    there = {by: jnp.logical_and(owner + by >= 0, owner + by < OWN) for by in (-2, -1, 1, 2)}
+    inner = jnp.logical_and(there[-1], there[1])
+
     def along(by):
         return (me, lax.rem(owner + by + OWN, OWN))
 
@@ -129,7 +152,7 @@
 
     barrier = pltpu.get_barrier_semaphore()
     for by in (-1, 1):
-        signal(barrier, along(by))
+        pl.when(there[by])(functools.partial(signal, barrier, along(by)))
     for by in range(1, FQ):
         signal(barrier, (lax.rem(me + by, FQ), owner))
 
@@ -150,25 +173,28 @@
             src_ref=src, dst_ref=dst, send_sem=send, recv_sem=recv, device_id=device, device_id_type=MESH
         )
 
+    def shift(src, dst, send, recv, by):
+        return Guarded(copy(src, dst, send, recv, along(by)), there[by], there[-by])
+
     def early(side, w):
         dst, by = ((from_right, -1), (from_left, 1))[side]
-        return copy(
-            white.at[:, w, :, pl.ds(0, F_PART), :], dst.at[:, w],
-            early_send.at[side, w], early_recv.at[side, w], along(by),
+        return shift(
+            white.at[:, w, :, pl.ds(0, F_PART), :], dst.at[:, w], early_send.at[side, w], early_recv.at[side, w], by
         )
 
     def early_relay(w):
-        return copy(
-            from_right.at[:, w], from_far.at[:, w], early_send.at[2, w], early_recv.at[2, w], along(-1)
-        )
+        sent = copy(from_right.at[:, w], from_far.at[:, w], early_send.at[2, w], early_recv.at[2, w], along(-1))
+        return Guarded(sent, inner, there[2])
 
     def regroup_more(i, by):
         peer = lax.rem(me + by, FQ)
         src = (from_left, from_right, from_far)[i]
-        return copy(
+        sent = copy(
             src.at[:, :, peer, :, :], more.at[i, by - 1],
             more_send.at[i, by - 1], more_recv.at[i, by - 1], (peer, owner),
         )
+        held_here = there[(-1, 1, 2)[i]]
+        return Guarded(sent, held_here, held_here)
 
     def part_bins(t):
         return pl.ds(pl.multiple_of(t * F_PART, F_PART), F_PART)
@@ -182,7 +208,7 @@
 
     def count_copies():
         return [
-            copy(counts.at[2], counts.at[to], cnt_send.at[i], cnt_recv.at[i], along(by))
+            shift(counts.at[2], counts.at[to], cnt_send.at[i], cnt_recv.at[i], by)
             for i, (to, by) in enumerate(((1, 1), (3, -1), (0, 2)))
         ]
 
@@ -190,19 +216,20 @@
         bins = pl.ds(t * F_PART + part * F_HALF, F_HALF)
         dst, by = ((right, -1), (left, 1))[side]
         at = 2 * t + part
-        return copy(held.at[bins], dst.at[bins], hop_send.at[side, at], hop_recv.at[side, at], along(by))
+        return shift(held.at[bins], dst.at[bins], hop_send.at[side, at], hop_recv.at[side, at], by)
 
     def relay(last, t, part):
         bins = pl.ds(t * F_PART + part * F_HALF, F_HALF)
         src, by = ((right, -1), (left, 1))[last]
         at = 2 * t + part
-        return copy(src.at[bins], far.at[bins], far_send.at[at], far_recv.at[at], along(by))
+        sent = copy(src.at[bins], far.at[bins], far_send.at[at], far_recv.at[at], along(by))
+        return Guarded(sent, inner, there[(2, -2)[last]])
 
     def returned(last, at, stage):
         bins = pl.ds(pl.multiple_of(at * F_HALF, F_HALF), F_HALF)
         plan = ((((2, 1, 1),), ((0, -1, 0), (3, 2, 2))), (((1, -1, 0),), ((3, 1, 1), (0, -2, 2))))[last][stage]
         return [
-            copy(sums.at[slot, bins, :], back.at[to, bins, :], ret_send.at[to, at], ret_recv.at[to, at], along(by))
+            shift(sums.at[slot, bins, :], back.at[to, bins, :], ret_send.at[to, at], ret_recv.at[to, at], by)
             for slot, by, to in plan
         ]
 
@@ -230,10 +257,55 @@
 
     def arrange_more(i):
         src = (from_left, from_right, from_far)[i]
-        place_part(
-            (left, right, far)[i], 0, lambda c, w: src[c, w, me], lambda by, c, w: more[i, by - 1, c, w],
-            lambda by: regroup_more(i, by).wait_recv(),
-        )
+
+        @pl.when(there[(-1, 1, 2)[i]])
+        def _():
+            place_part(
+                (left, right, far)[i], 0, lambda c, w: src[c, w, me], lambda by, c, w: more[i, by - 1, c, w],
+                lambda by: regroup_more(i, by).copy.wait_recv(),
+            )
+
+    def clear(ref, first_bin, bins):
+        @pl.loop(first_bin, first_bin + bins)
+        def _(f):
+            ref[f] = jnp.zeros(ref.shape[1:], ref.dtype)
+
+    def clear_units(ref, last):
+        for at in range(2 * T):
+            if LAST[at] == last:
+                clear(ref, at * F_HALF, F_HALF)
+
+    def clear_missing():
+        for by, near, back_at, count_at in ((-1, left, 1, 1), (1, right, 0, 3)):
+
+            @pl.when(jnp.logical_not(there[by]))
+            def _(near=near, back_at=back_at, count_at=count_at):
+                clear(near, 0, F_DEV)
+                back[back_at] = jnp.zeros((F_DEV, ST), jnp.float32)
+                counts[count_at] = jnp.zeros((16, SB), jnp.float32)
+
+        for by, last in ((-2, 1), (2, 0)):
+
+            @pl.when(jnp.logical_not(there[by]))
+            def _(last=last):
+                clear_units(far, last)
+                for at in range(2 * T):
+                    if LAST[at] != last:
+                        back[2, at * F_HALF : (at + 1) * F_HALF] = jnp.zeros((F_HALF, ST), jnp.float32)
+
+        @pl.when(jnp.logical_not(there[-2]))
+        def _():
+            counts[0] = jnp.zeros((16, SB), jnp.float32)
+
+    def compute_own(last):
+        def weight(p, q):
+            return counts[2, p * 8 + q : p * 8 + q + 1, :]
+
+        for run in ((2, 4), (5, 6), (7, 8)) if last else ((0, 2), (4, 5), (6, 7)):
+
+            @pl.loop(*run)
+            def _(at):
+                eight_bins(0, held, {0: held}, weight, pl.multiple_of(at * F_HALF, F_HALF), own)
 
     def start_hops(t):
         for side, part in ((0, 0), (1, 1), (0, 1), (1, 0)):
@@ -267,9 +339,13 @@
         loads[w].wait()
         whiten(spec, white, w, 1)
         if w == 0:
-            pl.semaphore_wait(barrier, FQ - 1 + 2)
-            signal(ready.at[0], along(1))
-            signal(ready.at[1], along(-1))
+            pl.semaphore_wait(barrier, FQ - 1 + there[-1].astype(jnp.int32) + there[1].astype(jnp.int32))
+
+            @pl.when(inner)
+            def _():
+                signal(ready.at[0], along(1))
+                signal(ready.at[1], along(-1))
+
         early(0, w).start()
         early(1, w).start()
     for t in (1, 2, 3, 0):
@@ -285,8 +361,12 @@
     for i in range(2):
         for by in range(1, FQ):
             regroup_more(i, by).start()
-    pl.semaphore_wait(ready.at[0], 1)
-    pl.semaphore_wait(ready.at[1], 1)
+    for i, by in ((0, -2), (1, 2)):
+
+        @pl.when(there[by])
+        def _(i=i):
+            pl.semaphore_wait(ready.at[i], 1)
+
     count_copies()[2].start()
 
     @pl.loop(2, T)
@@ -299,6 +379,7 @@
     for part in range(2):
         hop(1, 1, part).wait_recv()
         relay(1, 1, part).start()
+    clear_missing()
     for item in count_copies():
         item.wait_recv()
     hop(0, 1, 0).wait_recv()
@@ -324,6 +405,13 @@
         compute(0, 2 * t, 0)
         compute(1, 2 * t + 1, 0)
 
+    for by, last in ((-1, 1), (1, 0)):
+
+        @pl.when(jnp.logical_not(there[by]))
+        def _(last=last):
+            own[...] = jnp.zeros((1, F_DEV, ST), jnp.float32)
+            compute_own(last)
+
     for w in range(W_DEV):
         early_relay(w).wait_recv()
     for by in range(1, FQ):
@@ -355,6 +443,11 @@
             item.wait_recv()
         bins = slice(at * F_HALF, (at + 1) * F_HALF)
         out[bins] = (sums[1 + last, bins] + back[0, bins]) + (back[1, bins] + back[2, bins])
+
+    @pl.when(jnp.logical_not(inner))
+    def _():
+        out[...] += own[0]
+
     for t in range(T):
         for by in range(1, FQ):
             regroup(by, t).wait_send()
@@ -403,6 +496,7 @@
             pltpu.VMEM((4, 16, SB), jnp.float32),
             pltpu.VMEM((4, F_DEV, ST), jnp.float32),
             pltpu.VMEM((3, F_DEV, ST), jnp.float32),
+            pltpu.VMEM((1, F_DEV, ST), jnp.float32),
             dma((FQ - 1, T)), dma((FQ - 1, T)),
             dma((3, FQ - 1)), dma((3, FQ - 1)),
             dma((2, 2 * T)), dma((2, 2 * T)),

time: 81.2 us -> 76.3 us (0.940)
  the two profiles are of different devices: /device:TPU:1 before, /device:TPU:7 now
where the time goes in v3:
time: 76.3 us; the launch traced here: 76.1 us
  Pallas kernels  74.6 us (98%)
  local copies, waits for them, and re-layouts  1.47 us (2%)
    pallas_call x1, Pallas kernels, body(): pl.pallas_call(kernel, out_shape=jax.ShapeDtypeStruct((F_DEV, ST), jnp.fl...  74.6 us

profile of v3, /device:TPU:7, one launch (start us, length us, event | category | flops | bytes accessed | tf_op | source)
XLA Modules:
  0.0 76.1 jit_solution(12062329303410263278)
XLA Ops:
  0.0 74.6 %shard_map.37 = f32[64,256]{1,0:T(8,128)} custom-call(bf16[2,3,512,256]{3,2,1,0:T(8,128)(2,1)} %spec_hbm.1, s32[2,16]{1,0:T(2,128)} %bitcast.2, s32[1,16]{1,0:T(1,128)} %bitcast.3), custom_call_target="tpu_custom_call" | custom-call | flops 8000000000 | bytes 2097152 | tf_op jit(solution)/shard_map/pallas_call | solution.py:480
  74.6 1.5 %copy.5 = f32[64,256]{1,0:T(8,128)} copy(f32[64,256]{1,0:T(8,128)} %shard_map.37) | data formatting | bytes 131072

commit v4 on v3

--- a/solution.py
+++ b/solution.py
@@ -92,23 +92,36 @@
     return rows, {q: col.sum(axis=0, keepdims=True) for q, col in cols.items()}
 
 
-def eight_bins(anchor_slot, anchor, partners, weight, start, out):
+def eight_bins(units, out, waits=None):
     line = lax.broadcasted_iota(jnp.int32, (8, SB), 0)
-    near = anchor_slot in partners
-    own = [2 * anchor_slot, 2 * anchor_slot + 1]
-    keys = sorted({2 * s + h for s in partners for h in range(2)} | set(own))
+    keys = []
+    for anchor_slot, anchor, partners, weight, start in units:
+        own = [2 * anchor_slot, 2 * anchor_slot + 1]
+        keys.append(sorted({2 * s + h for s in partners for h in range(2)} | set(own)))
 
     def step(k, tiles):
-        rows, cols = one_bin(anchor, partners, weight, start + k)
-        for p in range(2):
-            cols[own[p]] = cols[own[p]] + rows[p] if near else rows[p]
-        return tuple(jnp.where(line == k, cols[q], tile) for q, tile in zip(keys, tiles))
+        result = []
+        for (anchor_slot, anchor, partners, weight, start), mine, old in zip(units, keys, tiles):
+            rows, cols = one_bin(anchor, partners, weight, start + k)
+            for p in range(2):
+                q = 2 * anchor_slot + p
+                cols[q] = cols[q] + rows[p] if anchor_slot in partners else rows[p]
+            result.append(tuple(jnp.where(line == k, cols[q], tile) for q, tile in zip(mine, old)))
+        return tuple(result)
 
     zero = jnp.zeros((8, SB), jnp.float32)
-    tiles = lax.fori_loop(0, 8, step, (zero,) * len(keys), unroll=UNROLL if len(partners) > 1 else 8)
-    for q, tile in zip(keys, tiles):
-        place = (q // 2, pl.ds(start, 8), slice((q % 2) * SB, (q % 2 + 1) * SB))
-        out[place] = tile if near or q not in own else out[place] + tile
+    tiles = tuple((zero,) * len(mine) for mine in keys)
+    if waits:
+        for half, wait in enumerate(waits):
+            wait()
+            tiles = lax.fori_loop(4 * half, 4 * half + 4, step, tiles, unroll=4)
+    else:
+        tiles = lax.fori_loop(0, 8, step, tiles, unroll=UNROLL if len(units[0][2]) > 1 else 8)
+    for (anchor_slot, anchor, partners, weight, start), mine, new in zip(units, keys, tiles):
+        for q, tile in zip(mine, new):
+            place = (q // 2, pl.ds(start, 8), slice((q % 2) * SB, (q % 2 + 1) * SB))
+            met = anchor_slot not in partners and q // 2 == anchor_slot
+            out[place] = out[place] + tile if met else tile
 
 
 class Guarded:
@@ -179,11 +192,11 @@
     def early(side, w):
         dst, by = ((from_right, -1), (from_left, 1))[side]
         return shift(
-            white.at[:, w, :, pl.ds(0, F_PART), :], dst.at[:, w], early_send.at[side, w], early_recv.at[side, w], by
+            white.at[:, w, :, pl.ds(0, F_PART), :], dst.at[:, w], early_send.at[side], early_recv.at[side, w], by
         )
 
     def early_relay(w):
-        sent = copy(from_right.at[:, w], from_far.at[:, w], early_send.at[2, w], early_recv.at[2, w], along(-1))
+        sent = copy(from_right.at[:, w], from_far.at[:, w], early_send.at[2], early_recv.at[2, w], along(-1))
         return Guarded(sent, inner, there[2])
 
     def regroup_more(i, by):
@@ -191,10 +204,14 @@
         src = (from_left, from_right, from_far)[i]
         sent = copy(
             src.at[:, :, peer, :, :], more.at[i, by - 1],
-            more_send.at[i, by - 1], more_recv.at[i, by - 1], (peer, owner),
+            more_send.at[i], more_recv.at[i], (peer, owner),
         )
         held_here = there[(-1, 1, 2)[i]]
         return Guarded(sent, held_here, held_here)
+
+    def regroup_more_all(i):
+        held_here = there[(-1, 1, 2)[i]]
+        return Guarded(copy(more.at[i], more.at[i], more_send.at[i], more_recv.at[i], (me, owner)), held_here, held_here)
 
     def part_bins(t):
         return pl.ds(pl.multiple_of(t * F_PART, F_PART), F_PART)
@@ -203,8 +220,12 @@
         peer = lax.rem(me + by, FQ)
         return copy(
             white.at[:, :, peer, part_bins(t), :], landed.at[by - 1, :, :, part_bins(t), :],
-            a2a_send.at[by - 1, t], a2a_recv.at[by - 1, t], (peer, owner),
+            a2a_send.at[0], a2a_recv.at[t], (peer, owner),
         )
+
+    def regroup_all(t):
+        bins = landed.at[:, :, :, part_bins(t), :]
+        return copy(bins, bins, a2a_send.at[0], a2a_recv.at[t], (me, owner))
 
     def count_copies():
         return [
@@ -215,28 +236,34 @@
     def hop(side, t, part):
         bins = pl.ds(t * F_PART + part * F_HALF, F_HALF)
         dst, by = ((right, -1), (left, 1))[side]
-        at = 2 * t + part
-        return shift(held.at[bins], dst.at[bins], hop_send.at[side, at], hop_recv.at[side, at], by)
-
-    def relay(last, t, part):
-        bins = pl.ds(t * F_PART + part * F_HALF, F_HALF)
+        at = 2 * t + part - 2
+        return shift(held.at[bins], dst.at[bins], hop_send.at[side], hop_recv.at[side, at], by)
+
+    def relay(last, t, part, half):
+        bins = pl.ds(t * F_PART + part * F_HALF + half * (F_HALF // 2), F_HALF // 2)
         src, by = ((right, -1), (left, 1))[last]
-        at = 2 * t + part
-        sent = copy(src.at[bins], far.at[bins], far_send.at[at], far_recv.at[at], along(by))
+        at = 4 * t + 2 * part + half - 4
+        sent = copy(src.at[bins], far.at[bins], far_send.at[0], far_recv.at[at], along(by))
         return Guarded(sent, inner, there[(2, -2)[last]])
 
     def returned(last, at, stage):
         bins = pl.ds(pl.multiple_of(at * F_HALF, F_HALF), F_HALF)
         plan = ((((2, 1, 1),), ((0, -1, 0), (3, 2, 2))), (((1, -1, 0),), ((3, 1, 1), (0, -2, 2))))[last][stage]
+        items = []
+        for slot, by, to in plan:
+            sem = to + last if to == 2 else to
+            items.append(shift(sums.at[slot, bins, :], back.at[to, bins, :], ret_send.at[sem], ret_recv.at[sem], by))
+        return items
+
+    def returned_all():
+        half = F_DEV // 2
         return [
-            shift(sums.at[slot, bins, :], back.at[to, bins, :], ret_send.at[to, at], ret_recv.at[to, at], by)
-            for slot, by, to in plan
+            shift(back.at[to, pl.ds(0, n), :], back.at[to, pl.ds(0, n), :], ret_send.at[i], ret_recv.at[i], by)
+            for i, (to, n, by) in enumerate(((0, F_DEV, -1), (1, F_DEV, 1), (2, half, 2), (2, half, -2)))
         ]
 
-    def place_part(dst, t, first, others, arrived):
+    def place_part(dst, t, first, others):
         for by in range(FQ):
-            if by:
-                arrived(by)
             for c in range(2):
                 for w in range(W_DEV):
                     k = c * WIN + by * W_DEV + w
@@ -250,9 +277,9 @@
 
     def arrange(t):
         bins = part_bins(t)
+        regroup_all(t).wait_recv()
         place_part(
-            held, t, lambda c, w: white[c, w, me, bins, :], lambda by, c, w: landed[by - 1, c, w, bins, :],
-            lambda by: regroup(by, t).wait_recv(),
+            held, t, lambda c, w: white[c, w, me, bins, :], lambda by, c, w: landed[by - 1, c, w, bins, :]
         )
 
     def arrange_more(i):
@@ -260,10 +287,8 @@
 
         @pl.when(there[(-1, 1, 2)[i]])
         def _():
-            place_part(
-                (left, right, far)[i], 0, lambda c, w: src[c, w, me], lambda by, c, w: more[i, by - 1, c, w],
-                lambda by: regroup_more(i, by).copy.wait_recv(),
-            )
+            regroup_more_all(i).copy.wait_recv()
+            place_part((left, right, far)[i], 0, lambda c, w: src[c, w, me], lambda by, c, w: more[i, by - 1, c, w])
 
     def clear(ref, first_bin, bins):
         @pl.loop(first_bin, first_bin + bins)
@@ -305,7 +330,7 @@
 
             @pl.loop(*run)
             def _(at):
-                eight_bins(0, held, {0: held}, weight, pl.multiple_of(at * F_HALF, F_HALF), own)
+                eight_bins([(0, held, {0: held}, weight, pl.multiple_of(at * F_HALF, F_HALF))], own)
 
     def start_hops(t):
         for side, part in ((0, 0), (1, 1), (0, 1), (1, 0)):
@@ -313,9 +338,10 @@
 
     def pass_on(t):
         hop(0, t, 0).wait_recv()
-        relay(0, t, 0).start()
         hop(1, t, 1).wait_recv()
-        relay(1, t, 1).start()
+        for half in range(2):
+            relay(0, t, 0, half).start()
+            relay(1, t, 1, half).start()
 
     def weight_first(p, q):
         return counts[1, p * 8 + q : p * 8 + q + 1, :]
@@ -324,15 +350,24 @@
         at = (q % 2) * 8 + 6 - 2 * (q // 2) + p
         return counts[q // 2, at : at + 1, :]
 
-    def compute(last, at, stage):
+    def unit(last, at, stage):
         start = pl.multiple_of(at * F_HALF, F_HALF)
         if last:
-            partners = {0: far} if stage else {1: left, 2: held, 3: right}
-            eight_bins(3, right, partners, weight_last, start, sums)
-        else:
-            partners = {3: far} if stage else {0: left, 1: held, 2: right}
-            eight_bins(0, left, partners, weight_first, start, sums)
+            return (3, right, {0: far} if stage else {1: left, 2: held, 3: right}, weight_last, start)
+        return (0, left, {3: far} if stage else {0: left, 1: held, 2: right}, weight_first, start)
+
+    def compute(last, at, stage):
+        eight_bins([unit(last, at, stage)], sums)
         for item in returned(last, at, stage):
+            item.start()
+
+    def compute_far(t):
+        def wait(half):
+            relay(0, t, 0, half).wait_recv()
+            relay(1, t, 1, half).wait_recv()
+
+        eight_bins([unit(0, 2 * t, 1), unit(1, 2 * t + 1, 1)], sums, [functools.partial(wait, half) for half in range(2)])
+        for item in returned(0, 2 * t, 1) + returned(1, 2 * t + 1, 1):
             item.start()
 
     for w in range(W_DEV):
@@ -378,7 +413,8 @@
         early_relay(w).start()
     for part in range(2):
         hop(1, 1, part).wait_recv()
-        relay(1, 1, part).start()
+        for half in range(2):
+            relay(1, 1, part, half).start()
     clear_missing()
     for item in count_copies():
         item.wait_recv()
@@ -419,15 +455,13 @@
 
     @pl.loop(2, 4)
     def _(at):
-        relay(1, 1, at - 2).wait_recv()
+        for half in range(2):
+            relay(1, 1, at - 2, half).wait_recv()
         compute(1, at, 1)
 
     @pl.loop(2, T)
     def _(t):
-        relay(0, t, 0).wait_recv()
-        compute(0, 2 * t, 1)
-        relay(1, t, 1).wait_recv()
-        compute(1, 2 * t + 1, 1)
+        compute_far(t)
 
         @pl.when(t == 2)
         def _():
@@ -437,37 +471,26 @@
             def _(at):
                 compute(0, at, 1)
 
+    for item in returned_all():
+        item.wait_recv()
     for at in range(2 * T):
-        last = LAST[at]
-        for item in returned(last, at, 0) + returned(last, at, 1):
-            item.wait_recv()
         bins = slice(at * F_HALF, (at + 1) * F_HALF)
-        out[bins] = (sums[1 + last, bins] + back[0, bins]) + (back[1, bins] + back[2, bins])
+        out[bins] = (sums[1 + LAST[at], bins] + back[0, bins]) + (back[1, bins] + back[2, bins])
 
     @pl.when(jnp.logical_not(inner))
     def _():
         out[...] += own[0]
 
-    for t in range(T):
-        for by in range(1, FQ):
-            regroup(by, t).wait_send()
-        for part in range(2):
-            at = 2 * t + part
-            last = LAST[at]
-            if t:
-                hop(0, t, part).wait_send()
-                hop(1, t, part).wait_send()
-                relay(last, t, part).wait_send()
-            for item in returned(last, at, 0) + returned(last, at, 1):
-                item.wait_send()
-    for w in range(W_DEV):
-        early(0, w).wait_send()
-        early(1, w).wait_send()
-        early_relay(w).wait_send()
+    copy(landed, landed, a2a_send.at[0], a2a_recv.at[0], (me, owner)).wait_send()
+    rest = pl.ds(F_PART, F_DEV - F_PART)
+    for side, by in ((0, -1), (1, 1)):
+        shift(held.at[rest], held.at[rest], hop_send.at[side], hop_recv.at[side, 0], by).wait_send()
+        shift(from_left, from_left, early_send.at[side], early_recv.at[side, 0], by).wait_send()
+    Guarded(copy(from_far, from_far, early_send.at[2], early_recv.at[2, 0], along(-1)), inner, inner).wait_send()
+    Guarded(copy(held.at[rest], far.at[rest], far_send.at[0], far_recv.at[0], along(-1)), inner, inner).wait_send()
     for i in range(3):
-        for by in range(1, FQ):
-            regroup_more(i, by).wait_send()
-    for item in count_copies():
+        regroup_more_all(i).wait_send()
+    for item in returned_all() + count_copies():
         item.wait_send()
 
 
@@ -497,13 +520,13 @@
             pltpu.VMEM((4, F_DEV, ST), jnp.float32),
             pltpu.VMEM((3, F_DEV, ST), jnp.float32),
             pltpu.VMEM((1, F_DEV, ST), jnp.float32),
-            dma((FQ - 1, T)), dma((FQ - 1, T)),
-            dma((3, FQ - 1)), dma((3, FQ - 1)),
-            dma((2, 2 * T)), dma((2, 2 * T)),
-            dma((2 * T,)), dma((2 * T,)),
+            dma((1,)), dma((T,)),
             dma((3,)), dma((3,)),
-            dma((3, 2 * T)), dma((3, 2 * T)),
-            dma((3, W_DEV)), dma((3, W_DEV)),
+            dma((2,)), dma((2, 2 * T - 2)),
+            dma((1,)), dma((4 * T - 4,)),
+            dma((3,)), dma((3,)),
+            dma((4,)), dma((4,)),
+            dma((3,)), dma((3, W_DEV)),
             pltpu.SemaphoreType.REGULAR((2,)),
         ],
         compiler_params=pltpu.CompilerParams(

time: 76.3 us -> 74 us (0.970)
  Pallas kernels: 74.6 us -> 72.4 us
    pallas_call x1, Pallas kernels: 74.6 us -> 72.4 us  [body(): pl.pallas_call(kernel, out_shape=jax.ShapeDtypeStruct((F_DEV, ST), jnp.fl...]
where the time goes in v4:
time: 74 us; the launch traced here: 73.9 us
  Pallas kernels  72.4 us (98%)
  local copies, waits for them, and re-layouts  1.47 us (2%)
    pallas_call x1, Pallas kernels, body(): pl.pallas_call(kernel, out_shape=jax.ShapeDtypeStruct((F_DEV, ST), jnp.fl...  72.4 us

profile of v4, /device:TPU:7, one launch (start us, length us, event | category | flops | bytes accessed | tf_op | source)
XLA Modules:
  0.0 73.9 jit_solution(7442423110929777405)
XLA Ops:
  0.0 72.4 %shard_map.37 = f32[64,256]{1,0:T(8,128)} custom-call(bf16[2,3,512,256]{3,2,1,0:T(8,128)(2,1)} %spec_hbm.1, s32[2,16]{1,0:T(2,128)} %bitcast.2, s32[1,16]{1,0:T(1,128)} %bitcast.3), custom_call_target="tpu_custom_call" | custom-call | flops 8000000000 | bytes 2097152 | tf_op jit(solution)/shard_map/pallas_call | solution.py:503
  72.4 1.5 %copy.5 = f32[64,256]{1,0:T(8,128)} copy(f32[64,256]{1,0:T(8,128)} %shard_map.37) | data formatting | bytes 131072

commit v5 on v4

--- a/solution.py
+++ b/solution.py
@@ -145,8 +145,8 @@
 
 
 def kernel(
-    spec_hbm, blocks_hbm, valid_hbm, out,
-    spec, blocks, valid, load_sem, white, from_left, from_right, from_far, landed, more, wide,
+    spec_hbm, slots, out,
+    spec, load_sem, white, from_left, from_right, from_far, landed, more, wide,
     held, left, right, far, counts, sums, back, own,
     a2a_send, a2a_recv, more_send, more_recv, hop_send, hop_recv, far_send, far_recv,
     cnt_send, cnt_recv, ret_send, ret_recv, early_send, early_recv, ready,
@@ -170,15 +170,11 @@
         signal(barrier, (lax.rem(me + by, FQ), owner))
 
     loads = [pltpu.make_async_copy(spec_hbm.at[:, w], spec.at[:, w], load_sem.at[w]) for w in range(W_DEV)]
-    loads.append(pltpu.make_async_copy(blocks_hbm, blocks, load_sem.at[W_DEV]))
-    loads.append(pltpu.make_async_copy(valid_hbm, valid, load_sem.at[W_DEV + 1]))
     for load in loads:
         load.start()
-    loads[W_DEV].wait()
-    loads[W_DEV + 1].wait()
     row = lax.broadcasted_iota(jnp.int32, (16, 16), 0)
-    place = (blocks[0:1, :] - 2 * owner) * 8 + (blocks[1:2, :] - 2 * owner)
-    table = jnp.sum(jnp.where(row == place, valid[...].astype(jnp.float32), 0.0), axis=1, keepdims=True)
+    place = slots[...] - 18 * owner
+    table = jnp.sum(jnp.where(row == place, 1.0, 0.0), axis=1, keepdims=True)
     counts[2] = jnp.broadcast_to(table * (1.0 / (WIN * SB)), (16, SB))
 
     def copy(src, dst, send, recv, device):
@@ -192,11 +188,11 @@
     def early(side, w):
         dst, by = ((from_right, -1), (from_left, 1))[side]
         return shift(
-            white.at[:, w, :, pl.ds(0, F_PART), :], dst.at[:, w], early_send.at[side], early_recv.at[side, w], by
+            white.at[:, w, :, pl.ds(0, F_PART), :], dst.at[:, w], early_send.at[side], early_recv.at[side], by
         )
 
     def early_relay(w):
-        sent = copy(from_right.at[:, w], from_far.at[:, w], early_send.at[2], early_recv.at[2, w], along(-1))
+        sent = copy(from_right.at[:, w], from_far.at[:, w], early_send.at[2], early_recv.at[2], along(-1))
         return Guarded(sent, inner, there[2])
 
     def regroup_more(i, by):
@@ -390,9 +386,8 @@
         item.start()
     arrange(1)
     start_hops(1)
-    for w in range(W_DEV):
-        early(0, w).wait_recv()
-        early(1, w).wait_recv()
+    for side, by in ((0, -1), (1, 1)):
+        shift(from_left, from_left, early_send.at[side], early_recv.at[side], by).wait_recv()
     for i in range(2):
         for by in range(1, FQ):
             regroup_more(i, by).start()
@@ -448,8 +443,7 @@
             own[...] = jnp.zeros((1, F_DEV, ST), jnp.float32)
             compute_own(last)
 
-    for w in range(W_DEV):
-        early_relay(w).wait_recv()
+    Guarded(copy(from_far, from_far, early_send.at[2], early_recv.at[2], along(-1)), there[2], there[2]).wait_recv()
     for by in range(1, FQ):
         regroup_more(2, by).start()
 
@@ -471,6 +465,17 @@
             def _(at):
                 compute(0, at, 1)
 
+    copy(landed, landed, a2a_send.at[0], a2a_recv.at[0], (me, owner)).wait_send()
+    rest = pl.ds(F_PART, F_DEV - F_PART)
+    for side, by in ((0, -1), (1, 1)):
+        shift(held.at[rest], held.at[rest], hop_send.at[side], hop_recv.at[side, 0], by).wait_send()
+        shift(from_left, from_left, early_send.at[side], early_recv.at[side], by).wait_send()
+    Guarded(copy(from_far, from_far, early_send.at[2], early_recv.at[2], along(-1)), inner, inner).wait_send()
+    Guarded(copy(held.at[rest], far.at[rest], far_send.at[0], far_recv.at[0], along(-1)), inner, inner).wait_send()
+    for i in range(3):
+        regroup_more_all(i).wait_send()
+    for item in count_copies():
+        item.wait_send()
     for item in returned_all():
         item.wait_recv()
     for at in range(2 * T):
@@ -481,21 +486,13 @@
     def _():
         out[...] += own[0]
 
-    copy(landed, landed, a2a_send.at[0], a2a_recv.at[0], (me, owner)).wait_send()
-    rest = pl.ds(F_PART, F_DEV - F_PART)
-    for side, by in ((0, -1), (1, 1)):
-        shift(held.at[rest], held.at[rest], hop_send.at[side], hop_recv.at[side, 0], by).wait_send()
-        shift(from_left, from_left, early_send.at[side], early_recv.at[side, 0], by).wait_send()
-    Guarded(copy(from_far, from_far, early_send.at[2], early_recv.at[2, 0], along(-1)), inner, inner).wait_send()
-    Guarded(copy(held.at[rest], far.at[rest], far_send.at[0], far_recv.at[0], along(-1)), inner, inner).wait_send()
-    for i in range(3):
-        regroup_more_all(i).wait_send()
-    for item in returned_all() + count_copies():
+    for item in returned_all():
         item.wait_send()
 
 
 def body(spectra, pair_blocks, pair_valid):
     dma = pltpu.SemaphoreType.DMA
+    slots = jnp.where(pair_valid == 1, pair_blocks[:, 0] * 8 + pair_blocks[:, 1], -1).reshape(1, 16)
     band = pltpu.VMEM((F_DEV, KDIM, ST), jnp.bfloat16)
     early = pltpu.VMEM((2, W_DEV, FQ, F_PART, ST), jnp.bfloat16)
     vmem = pl.BlockSpec(memory_space=pltpu.VMEM)
@@ -503,13 +500,11 @@
     return pl.pallas_call(
         kernel,
         out_shape=jax.ShapeDtypeStruct((F_DEV, ST), jnp.float32),
-        in_specs=[anywhere, anywhere, anywhere],
+        in_specs=[anywhere, vmem],
         out_specs=vmem,
         scratch_shapes=[
             pltpu.VMEM((2, W_DEV, FREQ, ST), jnp.bfloat16),
-            pltpu.VMEM((2, 16), jnp.int32),
-            pltpu.VMEM((1, 16), jnp.int32),
-            dma((W_DEV + 2,)),
+            dma((W_DEV,)),
             pltpu.VMEM((2, W_DEV, FQ, F_DEV, ST), jnp.bfloat16),
             early, early, early,
             pltpu.VMEM((FQ - 1, 2, W_DEV, F_DEV, ST), jnp.bfloat16),
@@ -526,14 +521,14 @@
             dma((1,)), dma((4 * T - 4,)),
             dma((3,)), dma((3,)),
             dma((4,)), dma((4,)),
-            dma((3,)), dma((3, W_DEV)),
+            dma((3,)), dma((3,)),
             pltpu.SemaphoreType.REGULAR((2,)),
         ],
         compiler_params=pltpu.CompilerParams(
-            collective_id=0, has_side_effects=True, vmem_limit_bytes=60 * 2**20
+            collective_id=0, has_side_effects=True, vmem_limit_bytes=53 * 2**20
         ),
         cost_estimate=pl.CostEstimate(flops=8 * 10**9, bytes_accessed=2 * 2**20, transcendentals=0),
-    )(spectra, pair_blocks.T, pair_valid.reshape(1, 16))
+    )(spectra, slots)
 
 
 def solution(mesh):

time: 74 us -> 73.2 us (0.989)
  local copies, waits for them, and re-layouts: 1.47 us -> 0.63 us
  other arithmetic: 0 us -> 0.76 us
    unnamed x1, local copies, waits for them, and re-layouts: 1.47 us -> 0.63 us
    reshape x0 -> x1, other arithmetic: none -> 0.76 us  [body(): jnp.where(pair_valid == 1, pair_blocks[:, 0] * 8 + pair_blocks[:, 1], -1)]
where the time goes in v5:
time: 73.2 us; the launch traced here: 73.1 us
  Pallas kernels  71.7 us (98%)
  other arithmetic  0.76 us (1%)
    pallas_call x1, Pallas kernels, body(): pl.pallas_call(kernel, out_shape=jax.ShapeDtypeStruct((F_DEV, ST), jnp.fl...  71.7 us

profile of v5, /device:TPU:7, one launch (start us, length us, event | category | flops | bytes accessed | tf_op | source)
XLA Modules:
  0.0 73.1 jit_solution(12872436055140650616)
XLA Ops:
  0.0 0.8 %fusion.slots = s32[1,16]{1,0:T(1,128)S(1)} fusion(s32[16]{0:T(128)} %param.5, s32[16,2]{0,1:T(2,128)} %param.4), kind=kLoop, calls=%fused_computation.1 | loop fusion | flops 64 | bytes 256 | tf_op jit(solution)/shard_map/reshape | solution.py:495
  0.8 71.7 %shard_map.37 = f32[64,256]{1,0:T(8,128)S(1)} custom-call(bf16[2,3,512,256]{3,2,1,0:T(8,128)(2,1)} %spec_hbm.1, s32[1,16]{1,0:T(1,128)S(1)} %fusion.slots), custom_call_target="tpu_custom_call" | custom-call | flops 8000000000 | bytes 2097152 | tf_op jit(solution)/shard_map/pallas_call | solution.py:500
  72.4 0.6 copy.5

commit v6 on v5

--- a/solution.py
+++ b/solution.py
@@ -24,6 +24,7 @@
 F_HALF = F_PART // 2
 KDIM = 2 * WIN
 UNROLL = 4
+PIECES = ((0, 6), (6, 8))
 LAST = (0, 0, 1, 1, 0, 1, 0, 1)
 
 
@@ -114,7 +115,8 @@
     if waits:
         for half, wait in enumerate(waits):
             wait()
-            tiles = lax.fori_loop(4 * half, 4 * half + 4, step, tiles, unroll=4)
+            first, end = PIECES[half]
+            tiles = lax.fori_loop(first, end, step, tiles, unroll=end - first)
     else:
         tiles = lax.fori_loop(0, 8, step, tiles, unroll=UNROLL if len(units[0][2]) > 1 else 8)
     for (anchor_slot, anchor, partners, weight, start), mine, new in zip(units, keys, tiles):
@@ -236,7 +238,7 @@
         return shift(held.at[bins], dst.at[bins], hop_send.at[side], hop_recv.at[side, at], by)
 
     def relay(last, t, part, half):
-        bins = pl.ds(t * F_PART + part * F_HALF + half * (F_HALF // 2), F_HALF // 2)
+        bins = pl.ds(t * F_PART + part * F_HALF + PIECES[half][0], PIECES[half][1] - PIECES[half][0])
         src, by = ((right, -1), (left, 1))[last]
         at = 4 * t + 2 * part + half - 4
         sent = copy(src.at[bins], far.at[bins], far_send.at[0], far_recv.at[at], along(by))

time: 73.2 us -> 73 us (level)
  no operation moved by 1% of the time
where the time goes in v6:
time: 73 us; the launch traced here: 72.9 us
  Pallas kernels  71.5 us (98%)
  other arithmetic  0.76 us (1%)
    pallas_call x1, Pallas kernels, body(): pl.pallas_call(kernel, out_shape=jax.ShapeDtypeStruct((F_DEV, ST), jnp.fl...  71.5 us

profile of v6, /device:TPU:7, one launch (start us, length us, event | category | flops | bytes accessed | tf_op | source)
XLA Modules:
  0.0 72.9 jit_solution(8837512714147899034)
XLA Ops:
  0.0 0.8 %fusion.slots = s32[1,16]{1,0:T(1,128)S(1)} fusion(s32[16]{0:T(128)} %param.5, s32[16,2]{0,1:T(2,128)} %param.4), kind=kLoop, calls=%fused_computation.1 | loop fusion | flops 64 | bytes 256 | tf_op jit(solution)/shard_map/reshape | solution.py:497
  0.8 71.5 %shard_map.37 = f32[64,256]{1,0:T(8,128)S(1)} custom-call(bf16[2,3,512,256]{3,2,1,0:T(8,128)(2,1)} %spec_hbm.1, s32[1,16]{1,0:T(1,128)S(1)} %fusion.slots), custom_call_target="tpu_custom_call" | custom-call | flops 8000000000 | bytes 2097152 | tf_op jit(solution)/shard_map/pallas_call | solution.py:502
  72.2 0.6 copy.5
